TPU v7x, 32 devices: a whole 2x2x4 slice. The times are simulated.
32 devices in a mesh: groups: 2 (over x), req: 2 (over core), tensor: 8 (over z, y).
Axes of the slice: x: 2, y: 2, z: 4, core: 2. Of those that a mesh axis runs over, the one named last changes fastest.
Arguments:
- hidden: bfloat16 [4096, 28672], P(('groups', 'req'), 'tensor'), parts along dimension 0, may hold values from -6 to 6
- down_matrix: bfloat16 [28672, 8192], P('tensor'), may hold values from -0.046875 to 0.046875
- shrink_factors: bfloat16 [64, 64, 28672], P('req', None, 'tensor'), may hold values from -0.03125 to 0.03125
- expand_factors: bfloat16 [64, 64, 8192], P('req', None, 'tensor'), may hold values from -0.75 to 0.75
- request_adapter: int32 [4, 8], P(('groups', 'req')), parts along dimension 0, may hold values from 0 to 63
- request_lengths: int32 [4, 8], P(('groups', 'req')), parts along dimension 0, may hold values from 1 to 512, 1024 in all within a row
- adapter_rank_table: int32 [64], replicated, may hold values from 16 to 64, as said below
- adapter_stored_row: int32 [64], replicated, may hold values from 0 to 63, each once
Outputs:
- layer_out: bfloat16 [4096, 8192], P(('groups', 'req'), 'tensor'), parts along dimension 0
There are 2 independent parts, one for each index of `groups`. A program takes and returns all parts, laid end to end along the dimension named above; an argument that names none is the same for every part. Nothing has to cross between parts.
Inputs may be any that keep to these rules, and one draw needn't show every extreme that they name: `adapter_rank_table`: every rank from 16 to 64 may occur; both ends occur in every draw. `request_lengths`: each row sums to 1024; its largest entry is exactly 512. `adapter_stored_row`: each stored row holds exactly one adapter.
All inputs are finite; a program needn't handle non-finite values.
Results may differ from a plain program's by a relative error of at most 0.004.
Values may be sent and summed in bfloat16 or wider, within the bound.
A program may use at most 256 MiB of HBM per device.

v0:
```python
import functools

import jax
import jax.numpy as jnp
from jax import lax
from jax.experimental import pallas as pl
from jax.experimental.pallas import tpu as pltpu
from jax.sharding import PartitionSpec as P

adapter_scale_factor = 16.0
ROWS = 256
MESH = pl.DeviceIdType.MESH
ZFIRST = 0


def lookup(values_table, id_list):
    matches = id_list[:, None] == jnp.arange(values_table.shape[0], dtype=jnp.int32)[None, :]
    return jnp.sum(jnp.where(matches, values_table[None, :], 0), axis=1)


def token_layout(request_lengths, req_count, tok_count):
    seg_ends = jnp.cumsum(request_lengths[0])
    positions = jnp.arange(tok_count, dtype=jnp.int32)
    req_of_tok = jnp.sum((positions[:, None] >= seg_ends[None, :]).astype(jnp.int32), axis=1)
    return req_of_tok[:, None] == jnp.arange(req_count, dtype=jnp.int32)[None, :]


def reduce_kernel(
    n_outer,
    rows,
    sub,
    hidden_hbm,
    down_hbm,
    out_hbm,
    hidden,
    tiles,
    y_send,
    y_got,
    own,
    z_got,
    load_sem,
    tile_sems,
    y_send_sem,
    y_got_sems,
    z_send_sem,
    z_got_sems,
    out_sem,
):
    tok_count = hidden.shape[0]
    pieces = tok_count // rows
    rounds = y_send.shape[0]
    chunks = rounds // pieces
    width = chunks * sub
    me = lax.axis_index("tensor")
    z, y = me // 2, me % 2
    last = n_outer - 1

    def device(index):
        return {"tensor": index}

    pair = z * 2 + (1 - y)
    above = (z + 1) * 2 + y
    below = (z - 1) * 2 + y

    def weights(dest_z, dest_y, chunk, slot):
        start = pl.multiple_of((dest_z * 2 + dest_y) * width + chunk * sub, 128)
        return pltpu.make_async_copy(
            down_hbm.at[:, pl.ds(start, sub)], tiles.at[slot], tile_sems.at[slot]
        )

    load = pltpu.make_async_copy(hidden_hbm, hidden, load_sem)
    load.start()
    weights(0, 1 - y, 0, 0).start()

    barrier = pltpu.get_barrier_semaphore()
    pl.semaphore_signal(barrier, inc=1, device_id=device(pair), device_id_type=MESH)

    @pl.when(z < last)
    def _():
        pl.semaphore_signal(barrier, inc=1, device_id=device(above), device_id_type=MESH)

    @pl.when(z > 0)
    def _():
        pl.semaphore_signal(barrier, inc=1, device_id=device(below), device_id_type=MESH)

    pl.semaphore_wait(barrier, 1 + jnp.minimum(z, 1) + jnp.minimum(last - z, 1))

    load.wait()

    def y_copy(rnd, dest):
        return pltpu.make_async_remote_copy(
            src_ref=y_send.at[rnd, dest],
            dst_ref=y_got.at[rnd, dest],
            send_sem=y_send_sem,
            recv_sem=y_got_sems.at[rnd, dest],
            device_id=device(pair),
            device_id_type=MESH,
        )

    def z_copy(rnd, dest, slot, target):
        return pltpu.make_async_remote_copy(
            src_ref=y_got.at[rnd, dest],
            dst_ref=z_got.at[rnd, slot],
            send_sem=z_send_sem,
            recv_sem=z_got_sems.at[rnd, slot],
            device_id=device(target),
            device_id_type=MESH,
        )

    def product(slot, piece):
        return jnp.dot(
            hidden[pl.ds(pl.multiple_of(piece * rows, rows), rows), :],
            tiles[slot],
            preferred_element_type=jnp.float32,
        )

    total_tiles = chunks * n_outer

    @pl.loop(0, total_tiles)
    def _(index):
        chunk, dest = index // n_outer, index % n_outer
        slot = index % 2

        @pl.when(index + 1 < total_tiles)
        def _():
            weights((index + 1) % n_outer, 1 - y, (index + 1) // n_outer, (index + 1) % 2).start()

        @pl.when(index + 1 == total_tiles)
        def _():
            weights(0, y, 0, total_tiles % 2).start()

        weights(dest, 1 - y, chunk, slot).wait()

        @pl.loop(0, pieces)
        def _(piece):
            rnd = chunk * pieces + piece
            y_send[rnd, dest] = product(slot, piece).astype(jnp.bfloat16)

            @pl.when(chunk == 0)
            def _():
                y_copy(rnd, dest).start()

        @pl.when((chunk > 0) & (dest == last))
        def _():
            @pl.loop(0, pieces * n_outer)
            def _(item):
                y_copy(chunk * pieces + item // n_outer, item % n_outer).start()

    def own_tiles(chunk):
        @pl.loop(0, n_outer)
        def _(dest):
            index = chunk * n_outer + dest
            slot = (total_tiles + index) % 2

            @pl.when(index + 1 < total_tiles)
            def _():
                weights(
                    (index + 1) % n_outer, y, (index + 1) // n_outer, (total_tiles + index + 1) % 2
                ).start()

            weights(dest, y, chunk, slot).wait()

            @pl.loop(0, pieces)
            def _(piece):
                own[chunk * pieces + piece, dest] = product(slot, piece)

    def out_copy(rnd):
        chunk, piece = rnd // pieces, rnd % pieces
        return pltpu.make_async_copy(
            own.at[rnd, z],
            out_hbm.at[
                pl.ds(pl.multiple_of(piece * rows, rows), rows),
                pl.ds(pl.multiple_of(chunk * sub, 128), sub),
            ],
            out_sem,
        )

    @pl.loop(0, rounds + last)
    def _(step):
        @pl.when((step < rounds) & (step % pieces == 0))
        def _():
            own_tiles(step // pieces)

        @pl.loop(0, n_outer)
        def _(dest):
            def pair_sum(rnd):
                y_copy(rnd, dest).wait_recv()
                own[rnd, dest] = own[rnd, dest] + y_got[rnd, dest].astype(jnp.float32)

            def add_line(rnd, slot):
                z_copy(rnd, dest, slot, pair).wait_recv()
                own[rnd, dest] = own[rnd, dest] + z_got[rnd, slot].astype(jnp.float32)

            up_round = step - z

            @pl.when((dest > z) & (up_round >= 0) & (up_round < rounds))
            def _():
                pair_sum(up_round)

                @pl.when(z > 0)
                def _():
                    add_line(up_round, dest)

                y_got[up_round, dest] = own[up_round, dest].astype(jnp.bfloat16)
                z_copy(up_round, dest, dest, above).start()

            down_round = step - (last - z)

            @pl.when((dest < z) & (down_round >= 0) & (down_round < rounds))
            def _():
                pair_sum(down_round)

                @pl.when(z < last)
                def _():
                    add_line(down_round, dest)

                y_got[down_round, dest] = own[down_round, dest].astype(jnp.bfloat16)
                slot = jnp.where(dest == z - 1, n_outer, dest)
                z_copy(down_round, dest, slot, below).start()

            end_round = step - jnp.maximum(z, last - z)

            @pl.when((dest == z) & (end_round >= 0) & (end_round < rounds))
            def _():
                pair_sum(end_round)

                @pl.when(z > 0)
                def _():
                    add_line(end_round, dest)

                @pl.when(z < last)
                def _():
                    add_line(end_round, n_outer)

                out_copy(end_round).start()

    pltpu.make_async_copy(y_send, y_got, y_send_sem).wait()

    if last > 0:
        moved = z_got.at[:, pl.ds(0, last)]
        pltpu.make_async_copy(moved, moved, z_send_sem).wait()

    pltpu.make_async_copy(out_hbm, out_hbm, out_sem).wait()


def reduced_product(hidden, down_matrix, n_tensor):
    tok_count, depth = hidden.shape
    total_width = down_matrix.shape[1]
    width = total_width // n_tensor
    n_outer = n_tensor // 2
    sub = min(256, width)
    rows = min(ROWS, tok_count)
    rounds = (width // sub) * (tok_count // rows)
    return pl.pallas_call(
        functools.partial(reduce_kernel, n_outer, rows, sub),
        out_shape=jax.ShapeDtypeStruct((tok_count, width), jnp.float32),
        in_specs=[pl.BlockSpec(memory_space=pl.ANY)] * 2,
        out_specs=pl.BlockSpec(memory_space=pl.ANY),
        scratch_shapes=[
            pltpu.VMEM((tok_count, depth), jnp.bfloat16),
            pltpu.VMEM((2, depth, sub), jnp.bfloat16),
            pltpu.VMEM((rounds, n_outer, rows, sub), jnp.bfloat16),
            pltpu.VMEM((rounds, n_outer, rows, sub), jnp.bfloat16),
            pltpu.VMEM((rounds, n_outer, rows, sub), jnp.float32),
            pltpu.VMEM((rounds, n_outer + 1, rows, sub), jnp.bfloat16),
            pltpu.SemaphoreType.DMA,
            pltpu.SemaphoreType.DMA((2,)),
            pltpu.SemaphoreType.DMA,
            pltpu.SemaphoreType.DMA((rounds, n_outer)),
            pltpu.SemaphoreType.DMA,
            pltpu.SemaphoreType.DMA((rounds, n_outer + 1)),
            pltpu.SemaphoreType.DMA,
        ],
        compiler_params=pltpu.CompilerParams(
            collective_id=0, has_side_effects=True, vmem_limit_bytes=62 * 1024 * 1024
        ),
        cost_estimate=pl.CostEstimate(
            flops=2 * tok_count * depth * total_width,
            bytes_accessed=2 * depth * total_width,
            transcendentals=0,
        ),
        name="reduced_product",
    )(hidden, down_matrix)


def fetch_rows(pool, my_slots, other_slots, half, size):
    per = pool.shape[0]
    low = half * per

    def local(slots):
        return pool[jnp.clip(slots - low, 0, per - 1)]

    rows = local(my_slots)
    got_rows = []
    for shift in range(1, size):
        pairs = [(r, (r - shift) % size) for r in range(size)]
        got_rows.append(lax.ppermute(local(other_slots[shift - 1]), "req", pairs))
    for shift in range(1, size):
        theirs = my_slots // per == (half + shift) % size
        rows = jnp.where(theirs[:, None, None], got_rows[shift - 1], rows)
    return rows


def make_per_device(n_tensor, n_req):
    def per_device(
        hidden,
        down_matrix,
        shrink_factors,
        expand_factors,
        request_adapter,
        request_lengths,
        adapter_rank_table,
        adapter_stored_row,
    ):
        tok_count = hidden.shape[0]
        req_count = request_adapter.shape[1]
        largest_rank = shrink_factors.shape[1]
        local_width = expand_factors.shape[2]
        half = lax.axis_index("req")
        all_ids = lax.all_gather(request_adapter[0], "req", axis=0)
        my_ids = request_adapter[0]
        my_ranks = lookup(adapter_rank_table, my_ids)
        my_slots = lookup(adapter_stored_row, my_ids)
        other_slots = [
            lookup(adapter_stored_row, all_ids[(half - shift) % n_req]) for shift in range(1, n_req)
        ]
        adapter_shrink_rows = fetch_rows(shrink_factors, my_slots, other_slots, half, n_req)
        adapter_expand_rows = fetch_rows(expand_factors, my_slots, other_slots, half, n_req)
        onehot = token_layout(request_lengths, req_count, tok_count)
        flat_a = adapter_shrink_rows.reshape(req_count * largest_rank, adapter_shrink_rows.shape[2])
        shrink_all = lax.dot_general(
            hidden, flat_a, (((1,), (1,)), ((), ())), preferred_element_type=jnp.float32
        )
        shrink_all = shrink_all.reshape(tok_count, req_count, largest_rank)
        live = jnp.arange(largest_rank, dtype=jnp.int32)[None, None, :] < my_ranks[None, :, None]
        keep_mask = onehot[:, :, None] & live
        shrink_result = jnp.sum(jnp.where(keep_mask, shrink_all, 0.0), axis=1)
        token_rank = jnp.sum(jnp.where(onehot, my_ranks[None, :], 0), axis=1)
        token_scale = adapter_scale_factor / token_rank.astype(jnp.float32)
        hidden, shrink_result = lax.optimization_barrier((hidden, shrink_result))
        folded = lax.psum(shrink_result.reshape(tok_count // 2, 2 * largest_rank), "tensor")
        base = reduced_product(hidden, down_matrix, n_tensor)
        scaled_result = (folded.reshape(tok_count, largest_rank) * token_scale[:, None]).astype(
            jnp.bfloat16
        )
        token_spread = jnp.where(
            onehot[:, :, None], scaled_result[:, None, :], jnp.zeros((), jnp.bfloat16)
        )
        token_spread = token_spread.reshape(tok_count, req_count * largest_rank)
        flattened_expand = adapter_expand_rows.reshape(req_count * largest_rank, local_width)
        adapter_piece = jnp.dot(token_spread, flattened_expand, preferred_element_type=jnp.float32)
        return (base + adapter_piece).astype(jnp.bfloat16)

    return per_device


def solution(mesh):
    in_specs = (
        P(("groups", "req"), "tensor"),
        P("tensor", None),
        P("req", None, "tensor"),
        P("req", None, "tensor"),
        P(("groups", "req"), None),
        P(("groups", "req"), None),
        P(),
        P(),
    )
    out_specs = P(("groups", "req"), "tensor")
    per_device = make_per_device(mesh.shape["tensor"], mesh.shape["req"])
    return jax.shard_map(
        per_device, mesh=mesh, in_specs=in_specs, out_specs=out_specs, check_vma=False
    )
```

profile of v0, /device:TPU:26, one launch (start us, length us, event | category | flops | bytes accessed | tf_op | source)
XLA Modules:
  0.0 261.6 jit_solution(669918821526691036)
XLA Ops:
  6.5 0.0 all-reduce.2.cloned.1.call-start
  6.5 1.9 all-gather
  8.4 0.9 select_reduce_fusion.4
  9.4 7.8 %gather_fusion = bf16[8,64,3584]{2,1,0:T(8,128)(2,1)} fusion(bf16[32,64,3584]{2,1,0:T(8,128)(2,1)} %param.10, s32[1024]{0:T(1024)S(1)} %pad_clamp_fusion.1), kind=kCustom, calls=%fused_computation | custom fusion | bytes 7340064 | tf_op jit(solution)/shard_map/gather | solution.py:291
  17.1 0.2 collective-permute-start
  17.3 2.8 %gather_fusion.2 = bf16[8,64,1024]{2,1,0:T(8,128)(2,1)S(1)} fusion(bf16[32,64,1024]{2,1,0:T(8,128)(2,1)} %param.11, s32[1024]{0:T(1024)S(1)} %pad_clamp_fusion.1), kind=kCustom, calls=%fused_computation.2 | custom fusion | bytes 2097184 | tf_op jit(solution)/shard_map/gather | solution.py:291
  20.1 0.4 collective-permute-start.1
  20.5 7.9 %gather_fusion.1 = bf16[8,64,3584]{2,1,0:T(8,128)(2,1)} fusion(bf16[32,64,3584]{2,1,0:T(8,128)(2,1)} %param.10, s32[1024]{0:T(1024)S(1)} %pad_clamp_fusion), kind=kCustom, calls=%fused_computation.1 | custom fusion | bytes 7340064 | tf_op jit(solution)/shard_map/gather | solution.py:291
  28.4 3.8 %gather_fusion.3 = bf16[8,64,1024]{2,1,0:T(8,128)(2,1)} fusion(bf16[32,64,1024]{2,1,0:T(8,128)(2,1)} %param.11, s32[1024]{0:T(1024)S(1)} %pad_clamp_fusion), kind=kCustom, calls=%fused_computation.3 | custom fusion | bytes 2097184 | tf_op jit(solution)/shard_map/gather | solution.py:291
  32.2 0.0 copy-done
  32.2 0.2 reduce-window.8
  32.4 0.1 convert_reduce_fusion
  32.4 0.1 select_reduce_fusion.1
  32.5 0.1 iota_compare_fusion.4
  32.6 0.0 collective-permute-done
  32.7 3.6 %broadcast_select_fusion = bf16[8,64,3584]{2,1,0:T(8,128)(2,1)S(1)} fusion(bf16[8,64,3584]{2,1,0:T(8,128)(2,1)} %collective-permute-done, bf16[8,64,3584]{2,1,0:T(8,128)(2,1)} %gather_fusion.1, pred[8]{0:T(512)(128)(4,1)S(1)} %fusion.9), kind=kLoop, calls=%fused_computation.6 | loop fusion | flops 1835008 | bytes 11010056 | tf_op jit(solution)/shard_map/jit(_where)/select_n | solution.py:300
  36.3 6.2 %fusion.11 = f32[512,1024]{1,0:T(8,128)S(1)} fusion(bf16[512,3584]{1,0:T(8,128)(2,1)S(1)} %bitcast.24, bf16[1024,3584]{1,0:T(8,128)(2,1)} %hidden_hbm), kind=kOutput, calls=%fused_computation.39 | convolution fusion | flops 3758096384 | bytes 13107200 | tf_op jit(solution)/shard_map/dot_general | solution.py:331
  42.5 1.1 select_reduce_fusion
  43.6 0.0 all-reduce.2.cloned.1.call-update
  43.6 204.6 %reduced_product.1 = f32[1024,1024]{1,0:T(8,128)} custom-call(bf16[1024,3584]{1,0:T(8,128)(2,1)} %hidden_hbm, bf16[3584,8192]{1,0:T(8,128)(2,1)} %down_hbm.1), custom_call_target="tpu_custom_call" | custom-call | flops 60129542144 | bytes 58720256 | tf_op jit(solution)/shard_map/reduced_product/pallas_call | solution.py:254
  248.2 0.0 all-reduce.2.cloned.1.call-done
  248.3 1.0 multiply_convert_fusion
  249.2 0.0 collective-permute-done.1
  249.2 5.5 %fusion = bf16[1024,1024]{1,0:T(8,128)(2,1)} fusion(f32[1024,1024]{1,0:T(8,128)} %reduced_product.1, bf16[8,64,1024]{2,1,0:T(8,128)(2,1)} %collective-permute-done.1, bf16[8,64,1024]{2,1,0:T(8,128)(2,1)} %gather_fusion.3, pred[8]{0:T(512)(128)(4,1)S(1)} %fusion.9, pred[1024,8]{0,1:T(8,128)(4,1)S(1)} %iota_compare_fusion, ...), kind=kOutput, calls=%fused_computation.5 | convolution fusion | flops 1076887552 | bytes 8527880 | tf_op jit(solution)/shard_map/dot_general | solution.py:351
  (8 shorter events, 0.1 us)
Async XLA Ops:
  6.5 241.7 %all-reduce.2.cloned.1.call-start = ((), (), s32[]{:S(2)}) async-start(), calls=%async_computation | async-start | bytes 524288 | tf_op jit(solution)/shard_map/psum | solution.py:341
  17.1 15.5 %collective-permute-start = (bf16[8,64,3584]{2,1,0:T(8,128)(2,1)}, bf16[8,64,3584]{2,1,0:T(8,128)(2,1)}, u32[]{:S(2)}, u32[]{:S(2)}) collective-permute-start(bf16[8,64,3584]{2,1,0:T(8,128)(2,1)} %gather_fusion), channel_id=1, source_target_pairs={{0,8},{8,0},{1,9},{9,1},{2,10},{10,2},{3,11},{11,3},{4,12},{12,4},... | collective-permute-start | bytes 11010056 | tf_op jit(solution)/shard_map/ppermute | solution.py:297
  20.1 229.1 %collective-permute-start.1 = (bf16[8,64,1024]{2,1,0:T(8,128)(2,1)S(1)}, bf16[8,64,1024]{2,1,0:T(8,128)(2,1)}, u32[]{:S(2)}, u32[]{:S(2)}) collective-permute-start(bf16[8,64,1024]{2,1,0:T(8,128)(2,1)S(1)} %gather_fusion.2), channel_id=1, source_target_pairs={{0,8},{8,0},{1,9},{9,1},{2,10},{10,2},{3,11},{11,3},{4,12},{12,4},... | collective-permute-start | bytes 3145736 | tf_op jit(solution)/shard_map/ppermute | solution.py:297
  20.5 11.7 %copy-start = (s32[1,8]{1,0:T(1,128)S(1)}, s32[1,8]{1,0:T(1,128)}, u32[]{:S(2)}) copy-start(s32[1,8]{1,0:T(1,128)} %param.13) | copy-start | bytes 100
Sparse Core Ops, SparseCore 0:
  43.7 71.5 all-reduce.1
where the time goes:
time: 262 us
  Pallas kernels  205 us (78%)
  local copies, waits for them, and re-layouts  22.2 us (8%)
  between operations  13.5 us (5%)
  matrix products  11.7 us (4%)
  other arithmetic  6.99 us (3%)
    pallas_call x1, Pallas kernels, reduced_product(): pl.pallas_call(functools.partial(reduce_kernel, n_outer, rows, sub), out_...  205 us
    gather x4, local copies, waits for them, and re-layouts, local(): return pool[jnp.clip(slots - low, 0, per - 1)]  22.2 us
    dot_general x1, matrix products, per_device(): lax.dot_general(hidden, flat_a, (((1,), (1,)), ((), ())), preferred_eleme...  6.24 us
    dot_general x1, matrix products, per_device(): jnp.dot(token_spread, flattened_expand, preferred_element_type=jnp.float32)  5.5 us
  transfers between devices with their start and end apart: 3, of which 0 were waited for; matrix products, arithmetic and copies ran while one was open for 10% of the time, Pallas kernels for 78%

commit v1 on v0

--- a/solution.py
+++ b/solution.py
@@ -9,6 +9,7 @@
 
 adapter_scale_factor = 16.0
 ROWS = 256
+DOT_ROWS = 1024
 MESH = pl.DeviceIdType.MESH
 ZFIRST = 0
 
@@ -107,12 +108,23 @@
             device_id_type=MESH,
         )
 
-    def product(slot, piece):
-        return jnp.dot(
-            hidden[pl.ds(pl.multiple_of(piece * rows, rows), rows), :],
-            tiles[slot],
-            preferred_element_type=jnp.float32,
-        )
+    group = min(pieces, DOT_ROWS // rows)
+
+    def product(slot, chunk, dest, store):
+        @pl.loop(0, pieces // group)
+        def _(part):
+            first = pl.multiple_of(part * group * rows, group * rows)
+            result = jnp.dot(
+                hidden[pl.ds(first, group * rows), :],
+                tiles[slot],
+                preferred_element_type=jnp.float32,
+            )
+            for piece in range(group):
+                store(
+                    chunk * pieces + part * group + piece,
+                    dest,
+                    result[piece * rows : (piece + 1) * rows],
+                )
 
     total_tiles = chunks * n_outer
 
@@ -131,14 +143,14 @@
 
         weights(dest, 1 - y, chunk, slot).wait()
 
-        @pl.loop(0, pieces)
-        def _(piece):
-            rnd = chunk * pieces + piece
-            y_send[rnd, dest] = product(slot, piece).astype(jnp.bfloat16)
+        def store_sent(rnd, dest, block):
+            y_send[rnd, dest] = block.astype(jnp.bfloat16)
 
             @pl.when(chunk == 0)
             def _():
                 y_copy(rnd, dest).start()
+
+        product(slot, chunk, dest, store_sent)
 
         @pl.when((chunk > 0) & (dest == last))
         def _():
@@ -146,6 +158,9 @@
             def _(item):
                 y_copy(chunk * pieces + item // n_outer, item % n_outer).start()
 
+    def store_own(rnd, dest, block):
+        own[rnd, dest] = block
+
     def own_tiles(chunk):
         @pl.loop(0, n_outer)
         def _(dest):
@@ -160,9 +175,7 @@
 
             weights(dest, y, chunk, slot).wait()
 
-            @pl.loop(0, pieces)
-            def _(piece):
-                own[chunk * pieces + piece, dest] = product(slot, piece)
+            product(slot, chunk, dest, store_own)
 
     def out_copy(rnd):
         chunk, piece = rnd // pieces, rnd % pieces
@@ -283,22 +296,57 @@
     )(hidden, down_matrix)
 
 
-def fetch_rows(pool, my_slots, other_slots, half, size):
-    per = pool.shape[0]
+def rows_kernel(slots, pool_a, pool_b, rows_a, rows_b):
+    rows_a[...] = pool_a[...]
+    rows_b[...] = pool_b[...]
+
+
+def local_rows(pool_a, pool_b, slots):
+    count = slots.shape[0]
+    block_a, block_b = (1,) + pool_a.shape[1:], (1,) + pool_b.shape[1:]
+    return pl.pallas_call(
+        rows_kernel,
+        out_shape=[
+            jax.ShapeDtypeStruct((count,) + pool_a.shape[1:], pool_a.dtype),
+            jax.ShapeDtypeStruct((count,) + pool_b.shape[1:], pool_b.dtype),
+        ],
+        grid_spec=pltpu.PrefetchScalarGridSpec(
+            num_scalar_prefetch=1,
+            grid=(count,),
+            in_specs=[
+                pl.BlockSpec(block_a, lambda step, slots: (slots[step], 0, 0)),
+                pl.BlockSpec(block_b, lambda step, slots: (slots[step], 0, 0)),
+            ],
+            out_specs=[
+                pl.BlockSpec(block_a, lambda step, slots: (step, 0, 0)),
+                pl.BlockSpec(block_b, lambda step, slots: (step, 0, 0)),
+            ],
+        ),
+        cost_estimate=pl.CostEstimate(
+            flops=0,
+            bytes_accessed=4 * count * (pool_a[0].size + pool_b[0].size),
+            transcendentals=0,
+        ),
+        name="local_rows",
+    )(slots, pool_a, pool_b)
+
+
+def fetch_rows(pool_a, pool_b, my_slots, other_slots, half, size):
+    per = pool_a.shape[0]
     low = half * per
 
     def local(slots):
-        return pool[jnp.clip(slots - low, 0, per - 1)]
-
-    rows = local(my_slots)
+        return local_rows(pool_a, pool_b, jnp.clip(slots - low, 0, per - 1))
+
     got_rows = []
     for shift in range(1, size):
         pairs = [(r, (r - shift) % size) for r in range(size)]
-        got_rows.append(lax.ppermute(local(other_slots[shift - 1]), "req", pairs))
+        got_rows.append([lax.ppermute(rows, "req", pairs) for rows in local(other_slots[shift - 1])])
+    both = local(my_slots)
     for shift in range(1, size):
-        theirs = my_slots // per == (half + shift) % size
-        rows = jnp.where(theirs[:, None, None], got_rows[shift - 1], rows)
-    return rows
+        theirs = (my_slots // per == (half + shift) % size)[:, None, None]
+        both = [jnp.where(theirs, got, rows) for got, rows in zip(got_rows[shift - 1], both)]
+    return both
 
 
 def make_per_device(n_tensor, n_req):
@@ -324,8 +372,9 @@
         other_slots = [
             lookup(adapter_stored_row, all_ids[(half - shift) % n_req]) for shift in range(1, n_req)
         ]
-        adapter_shrink_rows = fetch_rows(shrink_factors, my_slots, other_slots, half, n_req)
-        adapter_expand_rows = fetch_rows(expand_factors, my_slots, other_slots, half, n_req)
+        adapter_shrink_rows, adapter_expand_rows = fetch_rows(
+            shrink_factors, expand_factors, my_slots, other_slots, half, n_req
+        )
         onehot = token_layout(request_lengths, req_count, tok_count)
         flat_a = adapter_shrink_rows.reshape(req_count * largest_rank, adapter_shrink_rows.shape[2])
         shrink_all = lax.dot_general(

time: 262 us -> 255 us (0.973)
  local copies, waits for them, and re-layouts: 22.2 us -> 1.5 us
  Pallas kernels: 205 us -> 219 us
    gather x4 -> x0, local copies, waits for them, and re-layouts: 22.2 us -> none  [local(): return pool[jnp.clip(slots - low, 0, per - 1)]]
    pallas_call x0 -> x2, Pallas kernels: none -> 13.6 us  [local_rows(): pl.pallas_call(rows_kernel, out_shape=[jax.ShapeDtypeStruct((count,) + po...]
  transfers between devices with their start and end apart: 3 -> 3, of which waited for: 0 -> 1; matrix products, arithmetic and copies ran while one was open for 10% -> 4% of each run, Pallas kernels for 78% -> 84%
where the time goes in v1:
time: 255 us; the launch traced here: 254 us
  Pallas kernels  219 us (86%)
  between operations  13.5 us (5%)
  matrix products  9.16 us (4%)
  other arithmetic  7.7 us (3%)
    pallas_call x1, Pallas kernels, reduced_product(): pl.pallas_call(functools.partial(reduce_kernel, n_outer, rows, sub), out_...  206 us
    pallas_call x2, Pallas kernels, local_rows(): pl.pallas_call(rows_kernel, out_shape=[jax.ShapeDtypeStruct((count,) + po...  13.6 us
    dot_general x1, matrix products, per_device(): jnp.dot(token_spread, flattened_expand, preferred_element_type=jnp.float32)  5.19 us
  transfers between devices with their start and end apart: 3, of which 1 were waited for; matrix products, arithmetic and copies ran while one was open for 4% of the time, Pallas kernels for 84%

profile of v1, /device:TPU:26, one launch (start us, length us, event | category | flops | bytes accessed | tf_op | source)
XLA Modules:
  0.0 254.3 jit_solution(16467902524093346437)
XLA Ops:
  6.5 0.0 all-reduce.2.cloned.1.call-start
  6.5 1.9 all-gather
  8.4 0.9 select_reduce_fusion.4
  9.3 0.6 subtract_clamp_fusion
  9.9 6.4 %local_rows.2 = (bf16[8,64,3584]{2,1,0:T(8,128)(2,1)}, bf16[8,64,1024]{2,1,0:T(8,128)(2,1)}) custom-call(s32[8]{0:T(128)} %get-tuple-element.21.slots, bf16[32,64,3584]{2,1,0:T(8,128)(2,1)} %pool_a.3, bf16[32,64,1024]{2,1,0:T(8,128)(2,1)} %pool_b.3), custom_call_target="tpu_custom_call" | custom-call | bytes 9437184 | tf_op jit(solution)/shard_map/local_rows/pallas_call | solution.py:307
  16.3 1.3 collective-permute-start
  17.6 0.0 collective-permute-start.1
  17.7 7.2 %local_rows.3 = (bf16[8,64,3584]{2,1,0:T(8,128)(2,1)}, bf16[8,64,1024]{2,1,0:T(8,128)(2,1)}) custom-call(s32[8]{0:T(128)} %get-tuple-element.20.slots, bf16[32,64,3584]{2,1,0:T(8,128)(2,1)} %pool_a.3, bf16[32,64,1024]{2,1,0:T(8,128)(2,1)} %pool_b.3), custom_call_target="tpu_custom_call" | custom-call | bytes 9437184 | tf_op jit(solution)/shard_map/local_rows/pallas_call | solution.py:307
  24.9 0.0 copy-done.1
  24.9 0.2 reduce-window.8
  25.1 0.1 convert_reduce_fusion
  25.2 0.1 select_reduce_fusion.1
  25.3 0.1 iota_compare_fusion.4
  25.4 0.1 collective-permute-done
  25.5 3.7 %broadcast_select_fusion = bf16[8,64,3584]{2,1,0:T(8,128)(2,1)S(1)} fusion(bf16[8,64,3584]{2,1,0:T(8,128)(2,1)} %collective-permute-done, bf16[8,64,3584]{2,1,0:T(8,128)(2,1)} %get-tuple-element.12, pred[8]{0:T(512)(128)(4,1)S(1)} %fusion.7), kind=kLoop, calls=%fused_computation.2 | loop fusion | flops 1835008 | bytes 11010056 | tf_op jit(solution)/shard_map/jit(_where)/select_n | solution.py:348
  29.2 1.5 copy-done
  30.7 4.0 %fusion.9 = f32[512,1024]{1,0:T(8,128)S(1)} fusion(bf16[512,3584]{1,0:T(8,128)(2,1)S(1)} %bitcast.16, bf16[1024,3584]{1,0:T(8,128)(2,1)S(1)} %copy-done), kind=kOutput, calls=%fused_computation.31 | convolution fusion | flops 3758096384 | bytes 13107200 | tf_op jit(solution)/shard_map/dot_general | solution.py:380
  34.7 1.0 select_reduce_fusion
  35.8 0.0 all-reduce.2.cloned.1.call-update
  35.8 205.5 %reduced_product.1 = f32[1024,1024]{1,0:T(8,128)} custom-call(bf16[1024,3584]{1,0:T(8,128)(2,1)} %hidden_hbm, bf16[3584,8192]{1,0:T(8,128)(2,1)} %down_hbm.1), custom_call_target="tpu_custom_call" | custom-call | flops 60129542144 | bytes 58720256 | tf_op jit(solution)/shard_map/reduced_product/pallas_call | solution.py:267
  241.3 0.0 all-reduce.2.cloned.1.call-done
  241.3 1.0 multiply_convert_fusion
  242.3 0.0 collective-permute-done.1
  242.3 5.2 %fusion = bf16[1024,1024]{1,0:T(8,128)(2,1)} fusion(f32[1024,1024]{1,0:T(8,128)} %reduced_product.1, bf16[8,64,1024]{2,1,0:T(8,128)(2,1)S(1)} %collective-permute-done.1, bf16[8,64,1024]{2,1,0:T(8,128)(2,1)} %get-tuple-element.16, pred[8]{0:T(512)(128)(4,1)S(1)} %fusion.7, pred[1024,8]{0,1:T(8,128)(4,1)S(1)} %iota_compare_fusion, ...), kind=kOutput, calls=%fused_computation.1 | convolution fusion | flops 1076887552 | bytes 8527880 | tf_op jit(solution)/shard_map/dot_general | solution.py:400
  (6 shorter events, 0.0 us)
Async XLA Ops:
  6.5 234.8 %all-reduce.2.cloned.1.call-start = ((), (), s32[]{:S(2)}) async-start(), calls=%async_computation | async-start | bytes 524288 | tf_op jit(solution)/shard_map/psum | solution.py:390
  16.3 9.2 %collective-permute-start = (bf16[8,64,3584]{2,1,0:T(8,128)(2,1)}, bf16[8,64,3584]{2,1,0:T(8,128)(2,1)}, u32[]{:S(2)}, u32[]{:S(2)}) collective-permute-start(bf16[8,64,3584]{2,1,0:T(8,128)(2,1)} %get-tuple-element.11), channel_id=1, source_target_pairs={{0,8},{8,0},{1,9},{9,1},{2,10},{10,2},{3,11},{11,3},{4,12},{12,4},... | collective-permute-start | bytes 11010056 | tf_op jit(solution)/shard_map/ppermute | solution.py:344
  17.6 224.7 %collective-permute-start.1 = (bf16[8,64,1024]{2,1,0:T(8,128)(2,1)}, bf16[8,64,1024]{2,1,0:T(8,128)(2,1)S(1)}, u32[]{:S(2)}, u32[]{:S(2)}) collective-permute-start(bf16[8,64,1024]{2,1,0:T(8,128)(2,1)} %get-tuple-element.15), channel_id=1, source_target_pairs={{0,8},{8,0},{1,9},{9,1},{2,10},{10,2},{3,11},{11,3},{4,12},{12,4},... | collective-permute-start | bytes 3145736 | tf_op jit(solution)/shard_map/ppermute | solution.py:344
  17.7 7.2 %copy-start.1 = (s32[1,8]{1,0:T(1,128)S(1)}, s32[1,8]{1,0:T(1,128)}, u32[]{:S(2)}) copy-start(s32[1,8]{1,0:T(1,128)} %param.13) | copy-start | bytes 100
  25.5 5.2 %copy-start = (bf16[1024,3584]{1,0:T(8,128)(2,1)S(1)}, bf16[1024,3584]{1,0:T(8,128)(2,1)}, u32[]{:S(2)}) copy-start(bf16[1024,3584]{1,0:T(8,128)(2,1)} %hidden_hbm) | copy-start | bytes 22020100
Sparse Core Ops, SparseCore 0:
  35.9 72.1 all-reduce.1

commit v2 on v1

--- a/solution.py
+++ b/solution.py
@@ -197,8 +197,20 @@
         @pl.loop(0, n_outer)
         def _(dest):
             def pair_sum(rnd):
+                return own[rnd, dest] + y_got[rnd, dest].astype(jnp.float32)
+
+            def pass_on(rnd, first):
                 y_copy(rnd, dest).wait_recv()
-                own[rnd, dest] = own[rnd, dest] + y_got[rnd, dest].astype(jnp.float32)
+
+                @pl.when(first)
+                def _():
+                    y_got[rnd, dest] = pair_sum(rnd).astype(jnp.bfloat16)
+
+                @pl.when(jnp.logical_not(first))
+                def _():
+                    z_copy(rnd, dest, dest, pair).wait_recv()
+                    total = pair_sum(rnd) + z_got[rnd, dest].astype(jnp.float32)
+                    y_got[rnd, dest] = total.astype(jnp.bfloat16)
 
             def add_line(rnd, slot):
                 z_copy(rnd, dest, slot, pair).wait_recv()
@@ -208,26 +220,14 @@
 
             @pl.when((dest > z) & (up_round >= 0) & (up_round < rounds))
             def _():
-                pair_sum(up_round)
-
-                @pl.when(z > 0)
-                def _():
-                    add_line(up_round, dest)
-
-                y_got[up_round, dest] = own[up_round, dest].astype(jnp.bfloat16)
+                pass_on(up_round, z == 0)
                 z_copy(up_round, dest, dest, above).start()
 
             down_round = step - (last - z)
 
             @pl.when((dest < z) & (down_round >= 0) & (down_round < rounds))
             def _():
-                pair_sum(down_round)
-
-                @pl.when(z < last)
-                def _():
-                    add_line(down_round, dest)
-
-                y_got[down_round, dest] = own[down_round, dest].astype(jnp.bfloat16)
+                pass_on(down_round, z == last)
                 slot = jnp.where(dest == z - 1, n_outer, dest)
                 z_copy(down_round, dest, slot, below).start()
 
@@ -235,7 +235,8 @@
 
             @pl.when((dest == z) & (end_round >= 0) & (end_round < rounds))
             def _():
-                pair_sum(end_round)
+                y_copy(end_round, dest).wait_recv()
+                own[end_round, dest] = pair_sum(end_round)
 
                 @pl.when(z > 0)
                 def _():

time: 255 us -> 254 us (level)
  transfers between devices with their start and end apart: 3 -> 3, of which waited for: 1 -> 0; matrix products, arithmetic and copies ran while one was open for 4% -> 4% of each run, Pallas kernels for 84% -> 84%
where the time goes in v2:
time: 254 us
  Pallas kernels  220 us (87%)
  between operations  13.5 us (5%)
  matrix products  9.16 us (4%)
  other arithmetic  7.7 us (3%)
    pallas_call x1, Pallas kernels, reduced_product(): pl.pallas_call(functools.partial(reduce_kernel, n_outer, rows, sub), out_...  205 us
    pallas_call x2, Pallas kernels, local_rows(): pl.pallas_call(rows_kernel, out_shape=[jax.ShapeDtypeStruct((count,) + po...  15.1 us
    dot_general x1, matrix products, per_device(): jnp.dot(token_spread, flattened_expand, preferred_element_type=jnp.float32)  5.19 us
  transfers between devices with their start and end apart: 3, of which 0 were waited for; matrix products, arithmetic and copies ran while one was open for 4% of the time, Pallas kernels for 84%

profile of v2, /device:TPU:26, one launch (start us, length us, event | category | flops | bytes accessed | tf_op | source)
XLA Modules:
  0.0 254.1 jit_solution(6642904520050960829)
XLA Ops:
  6.5 1.9 all-gather
  8.4 0.9 select_reduce_fusion.4
  9.3 0.6 subtract_clamp_fusion
  9.9 7.5 %local_rows.2 = (bf16[8,64,3584]{2,1,0:T(8,128)(2,1)}, bf16[8,64,1024]{2,1,0:T(8,128)(2,1)}) custom-call(s32[8]{0:T(128)} %get-tuple-element.21.slots, bf16[32,64,3584]{2,1,0:T(8,128)(2,1)} %pool_a.3, bf16[32,64,1024]{2,1,0:T(8,128)(2,1)} %pool_b.3), custom_call_target="tpu_custom_call" | custom-call | bytes 9437184 | tf_op jit(solution)/shard_map/local_rows/pallas_call | solution.py:308
  17.4 0.0 collective-permute-start
  17.4 0.5 collective-permute-start.1
  17.9 7.6 %local_rows.3 = (bf16[8,64,3584]{2,1,0:T(8,128)(2,1)}, bf16[8,64,1024]{2,1,0:T(8,128)(2,1)}) custom-call(s32[8]{0:T(128)} %get-tuple-element.20.slots, bf16[32,64,3584]{2,1,0:T(8,128)(2,1)} %pool_a.3, bf16[32,64,1024]{2,1,0:T(8,128)(2,1)} %pool_b.3), custom_call_target="tpu_custom_call" | custom-call | bytes 9437184 | tf_op jit(solution)/shard_map/local_rows/pallas_call | solution.py:308
  25.6 0.0 copy-done.1
  25.6 0.2 reduce-window.8
  25.8 0.1 convert_reduce_fusion
  25.8 0.1 select_reduce_fusion.1
  25.9 0.1 iota_compare_fusion.4
  26.0 0.0 collective-permute-done
  26.1 0.0 copy-start
  26.1 3.7 %broadcast_select_fusion = bf16[8,64,3584]{2,1,0:T(8,128)(2,1)S(1)} fusion(bf16[8,64,3584]{2,1,0:T(8,128)(2,1)} %collective-permute-done, bf16[8,64,3584]{2,1,0:T(8,128)(2,1)} %get-tuple-element.12, pred[8]{0:T(512)(128)(4,1)S(1)} %fusion.7), kind=kLoop, calls=%fused_computation.2 | loop fusion | flops 1835008 | bytes 11010056 | tf_op jit(solution)/shard_map/jit(_where)/select_n | solution.py:349
  29.8 1.5 copy-done
  31.3 4.0 %fusion.9 = f32[512,1024]{1,0:T(8,128)S(1)} fusion(bf16[512,3584]{1,0:T(8,128)(2,1)S(1)} %bitcast.16, bf16[1024,3584]{1,0:T(8,128)(2,1)S(1)} %copy-done), kind=kOutput, calls=%fused_computation.31 | convolution fusion | flops 3758096384 | bytes 13107200 | tf_op jit(solution)/shard_map/dot_general | solution.py:381
  35.3 1.0 select_reduce_fusion
  36.3 0.0 all-reduce.2.cloned.1.call-update
  36.3 204.7 %reduced_product.1 = f32[1024,1024]{1,0:T(8,128)} custom-call(bf16[1024,3584]{1,0:T(8,128)(2,1)} %hidden_hbm, bf16[3584,8192]{1,0:T(8,128)(2,1)} %down_hbm.1), custom_call_target="tpu_custom_call" | custom-call | flops 60129542144 | bytes 58720256 | tf_op jit(solution)/shard_map/reduced_product/pallas_call | solution.py:268
  241.1 0.0 all-reduce.2.cloned.1.call-done
  241.1 1.0 multiply_convert_fusion
  242.1 0.0 collective-permute-done.1
  242.1 5.2 %fusion = bf16[1024,1024]{1,0:T(8,128)(2,1)} fusion(f32[1024,1024]{1,0:T(8,128)} %reduced_product.1, bf16[8,64,1024]{2,1,0:T(8,128)(2,1)S(1)} %collective-permute-done.1, bf16[8,64,1024]{2,1,0:T(8,128)(2,1)} %get-tuple-element.16, pred[8]{0:T(512)(128)(4,1)S(1)} %fusion.7, pred[1024,8]{0,1:T(8,128)(4,1)S(1)} %iota_compare_fusion, ...), kind=kOutput, calls=%fused_computation.1 | convolution fusion | flops 1076887552 | bytes 8527880 | tf_op jit(solution)/shard_map/dot_general | solution.py:401
  (6 shorter events, 0.0 us)
Async XLA Ops:
  6.5 234.5 %all-reduce.2.cloned.1.call-start = ((), (), s32[]{:S(2)}) async-start(), calls=%async_computation | async-start | bytes 524288 | tf_op jit(solution)/shard_map/psum | solution.py:391
  17.4 8.6 %collective-permute-start = (bf16[8,64,3584]{2,1,0:T(8,128)(2,1)}, bf16[8,64,3584]{2,1,0:T(8,128)(2,1)}, u32[]{:S(2)}, u32[]{:S(2)}) collective-permute-start(bf16[8,64,3584]{2,1,0:T(8,128)(2,1)} %get-tuple-element.11), channel_id=1, source_target_pairs={{0,8},{8,0},{1,9},{9,1},{2,10},{10,2},{3,11},{11,3},{4,12},{12,4},... | collective-permute-start | bytes 11010056 | tf_op jit(solution)/shard_map/ppermute | solution.py:345
  17.4 224.6 %collective-permute-start.1 = (bf16[8,64,1024]{2,1,0:T(8,128)(2,1)}, bf16[8,64,1024]{2,1,0:T(8,128)(2,1)S(1)}, u32[]{:S(2)}, u32[]{:S(2)}) collective-permute-start(bf16[8,64,1024]{2,1,0:T(8,128)(2,1)} %get-tuple-element.15), channel_id=1, source_target_pairs={{0,8},{8,0},{1,9},{9,1},{2,10},{10,2},{3,11},{11,3},{4,12},{12,4},... | collective-permute-start | bytes 3145736 | tf_op jit(solution)/shard_map/ppermute | solution.py:345
  17.9 7.6 %copy-start.1 = (s32[1,8]{1,0:T(1,128)S(1)}, s32[1,8]{1,0:T(1,128)}, u32[]{:S(2)}) copy-start(s32[1,8]{1,0:T(1,128)} %param.13) | copy-start | bytes 100
  26.1 5.2 %copy-start = (bf16[1024,3584]{1,0:T(8,128)(2,1)S(1)}, bf16[1024,3584]{1,0:T(8,128)(2,1)}, u32[]{:S(2)}) copy-start(bf16[1024,3584]{1,0:T(8,128)(2,1)} %hidden_hbm) | copy-start | bytes 22020100
Sparse Core Ops, SparseCore 0:
  36.5 71.4 all-reduce.1
